TPU v7x, 512 devices: a whole 4x4x16 slice. The times are simulated.
512 devices in a mesh: aper: 32 (over z, core), rng: 4 (over x), ang: 4 (over y).
Axes of the slice: x: 4, y: 4, z: 16, core: 2. Of those that a mesh axis runs over, the one named last changes fastest.
Arguments:
- subimages: bfloat16 [128, 2, 1024, 512], P('aper', None, 'ang', 'rng'), may hold values from -6 to 6
- beam_offsets: int32 [3, 2, 2, 1024], P(None, None, None, 'ang'), may hold values from -4 to 0
- range_offsets: int32 [3, 2, 2, 1024], P(None, None, None, 'ang'), may hold values from -4 to 3
- beam_taps: bfloat16 [3, 2, 2, 4, 1024], P(None, None, None, None, 'ang'), may hold values from 0.14941406 to 0.59765625
- range_frac: float32 [3, 2, 2, 1024], P(None, None, None, 'ang'), may hold values from 0 to 1
- phase_base: float32 [128, 3, 2, 1024], P('aper', None, None, 'ang'), may hold values from -3.140625 to 3.140625
- phase_rate: float32 [3, 2, 1024], P(None, None, 'ang'), may hold values from -6 to 6
- final_phase: float32 [128, 1024], P(None, 'ang'), may hold values from -3.140625 to 3.140625
Outputs:
- image: float32 [2, 4, 256, 512], P(None, 'ang', 'aper', 'rng')
Inputs may be any that keep to these rules, and one draw needn't show every extreme that they name: `beam_offsets`: the taps of parent beam p read child beams p + offset to p + offset + 3. `range_offsets`: range bin r reads the bins r + offset and r + offset + 1.
All inputs are finite; a program needn't handle non-finite values.
Results may differ from a plain program's by a relative error of at most 0.0046.
Values may be sent and summed in bfloat16 or wider, within the bound.
A program may use at most 64 MiB of HBM per device.

v0:
```python
import functools
import math

import jax
import jax.numpy as jnp
from jax import lax
from jax.experimental import pallas as pl
from jax.experimental.pallas import tpu as pltpu
from jax.sharding import PartitionSpec as P

MESH = pl.DeviceIdType.MESH
F32 = jnp.float32
BF16 = jnp.bfloat16
I32 = jnp.int32

ROWS_BELOW_IN = (16, 8, 4)
ROWS_BELOW_OUT = (8, 4, 0)
ROWS_IN = (160, 144, 144)
ROWS_OUT = (144, 144, 128)
NT = (((1,), (1,)), ((), ()))

SIN_C = (0.9999999957158404, -0.16666657969904627, 0.008333050617327633, -0.0001980904635743576, 2.605166275944652e-06)
COS_C = (0.9999999997799074, -0.49999999356956554, 0.04166663620892635, -0.0013888360842520568, 2.4760135515714637e-05, -2.605107635999247e-07)


def cos_sin(angle):
    turns = jnp.floor(angle * (0.5 / math.pi) + 0.5)
    rest = (angle - turns * 6.28125) - turns * (2 * math.pi - 6.28125)
    half = 0.5 * rest
    sq = half * half
    s = jnp.full_like(sq, SIN_C[-1])
    for coef in SIN_C[-2::-1]:
        s = s * sq + coef
    s = s * half
    c = jnp.full_like(sq, COS_C[-1])
    for coef in COS_C[-2::-1]:
        c = c * sq + coef
    return 1.0 - 2.0 * s * s, 2.0 * s * c


def lane_of(shape):
    return lax.broadcasted_iota(I32, shape, len(shape) - 1)


def row_of(shape):
    return lax.broadcasted_iota(I32, shape, len(shape) - 2)


def dot(a, b):
    return jnp.dot(a, b, preferred_element_type=F32)


def shift_rows(range_offset, fraction):
    o = range_offset + 4.0
    b4 = jnp.where(o >= 4.0, 1.0, 0.0)
    o = o - 4.0 * b4
    b2 = jnp.where(o >= 2.0, 1.0, 0.0)
    b1 = o - 2.0 * b2
    return b4, b2, (1.0 - b1) * (1.0 - fraction), (1.0 - b1) * fraction + b1 * (1.0 - fraction), b1 * fraction


def tap_matrix(lag, taps):
    out = jnp.where(lag == 3.0, taps[3], 0.0)
    for t in (2, 1, 0):
        out = jnp.where(lag == float(t), taps[t], out)
    return out


def kernel(
    sub, bo, ro, bt, rf, pb, pr, fp, out,
    XM, PE, PH, TAB, TABH, PS, PB2, PB1, PB0, PB1H, PB0H,
    RHS, RHSH0, RHSH1, WT, WTH, EM, EH, PC2, PC1, PC0, PCH,
    L0, L1, L2, IB, IH, S2, S2H, HB, ACC, FB, SB, RS,
    ssem, rsem, rs_ssem, rs_rsem,
):
    A = lax.axis_index("aper")
    X = lax.axis_index("rng")
    Y = lax.axis_index("ang")
    top = A // 4
    low = A % 4
    c2 = top // 4
    c1 = (top // 2) % 2
    c0 = top % 2
    cbits = (c0, c1, c2)
    t2 = c2
    t10 = top % 4

    barrier = pltpu.get_barrier_semaphore()

    def tell(**where):
        pl.semaphore_signal(barrier, inc=1, device_id=where, device_id_type=MESH)

    def tell_aper(k, carry):
        tell(aper=(A + k) % 32)
        return carry

    lax.fori_loop(1, 32, tell_aper, 0)
    y_ok = (Y > 0, Y < 3)
    x_ok = (X > 0, X < 3)
    for dy, ok_y in ((-1, y_ok[0]), (1, y_ok[1])):
        @pl.when(ok_y)
        def _():
            for q in range(4):
                tell(aper=4 * (t2 * 4 + q) + low, ang=Y + dy)
    for dx, ok_x in ((-1, x_ok[0]), (1, x_ok[1])):
        @pl.when(ok_x)
        def _():
            tell(rng=X + dx)
        for dy, ok_y in ((-1, y_ok[0]), (1, y_ok[1])):
            @pl.when(jnp.logical_and(ok_x, ok_y))
            def _():
                tell(rng=X + dx, ang=Y + dy)
    one = lambda ok: jnp.where(ok, 1, 0).astype(I32)
    ny = one(y_ok[0]) + one(y_ok[1])
    nx = one(x_ok[0]) + one(x_ok[1])

    eye = jnp.where(row_of((128, 128)) == lane_of((128, 128)), 1.0, 0.0).astype(BF16)
    for j in range(4):
        for ri in range(2):
            turned = lax.dot_general(eye, sub[j, ri], NT, preferred_element_type=F32).astype(BF16)
            XM[2 * j + ri, 0, 16:144, :] = turned[:, 0:128]
            XM[2 * j + ri, 1, 16:144, :] = turned[:, 128:256]
    for side, first in ((0, 0), (1, 240)):
        edge = sub[:, :, first:first + 16, :].reshape(128, 128)
        PE[side] = lax.dot_general(eye, edge, NT, preferred_element_type=F32).astype(BF16)

    for lvl in range(3):
        c = cbits[lvl]
        offs = bo[lvl, c].astype(F32)
        rofs = ro[lvl, c].astype(F32)
        frac = rf[lvl, c]
        taps = bt[lvl, c].astype(F32)
        rates = pr[lvl]
        rate = jnp.where(c == 0, rates[0:1], rates[1:2])
        for b in range(2):
            cut = slice(128 * b, 128 * b + 128)
            r0 = 16 * lvl
            TAB[b, r0:r0 + 2, :] = offs[:, cut]
            TAB[b, r0 + 2:r0 + 4, :] = rofs[:, cut]
            TAB[b, r0 + 4:r0 + 6, :] = frac[:, cut]
            TAB[b, r0 + 6:r0 + 7, :] = rate[:, cut]
            TAB[b, r0 + 7:r0 + 8, :] = rate[:, cut]
            TAB[b, r0 + 8:r0 + 12, :] = taps[0, :, cut]
            TAB[b, r0 + 12:r0 + 16, :] = taps[1, :, cut]
    for j in range(4):
        for lvl in range(3):
            base = pb[j, lvl]
            for c in range(2):
                for b in range(2):
                    PS[lvl, c, b, j:j + 1, :] = base[c:c + 1, 128 * b:128 * b + 128]
    PB2[top] = PS[2, c2]
    PB1[t10] = PS[1, c1]
    PB0[c0] = PS[0, c0]
    SHARED = 32

    @pl.when(X == 0)
    def _():
        XM[:, :, 0:16, :] = jnp.zeros((8, 2, 16, 128), BF16)
        PH[:, 0:16, :] = jnp.zeros((2, 16, 128), BF16)

    @pl.when(X == 3)
    def _():
        XM[:, :, 144:160, :] = jnp.zeros((8, 2, 16, 128), BF16)
        PH[:, 144:160, :] = jnp.zeros((2, 16, 128), BF16)

    for side, edge_at in ((0, 0), (1, 3)):
        @pl.when(Y == edge_at)
        def _():
            PH[side] = jnp.zeros((160, 128), BF16)
            TABH[side] = jnp.zeros((SHARED, 128), F32)
            PB1H[side] = jnp.zeros((4, 4, 128), F32)
            PB0H[side] = jnp.zeros((2, 4, 128), F32)

    copies = []
    count = [0]

    def plan(src, dst, slot, send_if, take_if, **where):
        copies.append((
            send_if, take_if,
            pltpu.make_async_remote_copy(
                src_ref=src, dst_ref=dst, send_sem=ssem.at[count[0]], recv_sem=rsem.at[slot],
                device_id=where, device_id_type=MESH,
            ),
        ))
        count[0] += 1

    plan(XM.at[:, :, pl.ds(128, 16), :], XM.at[:, :, pl.ds(0, 16), :], 0, x_ok[1], x_ok[0], rng=X + 1)
    plan(XM.at[:, :, pl.ds(16, 16), :], XM.at[:, :, pl.ds(144, 16), :], 1, x_ok[0], x_ok[1], rng=X - 1)
    both = jnp.logical_and
    for side in range(2):
        dy = 1 - 2 * side
        send_y, take_y = y_ok[1 - side], y_ok[side]
        edge = PE.at[1 - side]
        plan(edge, PH.at[side, pl.ds(16, 128), :], 2 + side, send_y, take_y, ang=Y + dy)
        plan(edge.at[pl.ds(112, 16), :], PH.at[side, pl.ds(0, 16), :], 4 + side,
             both(send_y, x_ok[1]), both(take_y, x_ok[0]), rng=X + 1, ang=Y + dy)
        plan(edge.at[pl.ds(0, 16), :], PH.at[side, pl.ds(144, 16), :], 6 + side,
             both(send_y, x_ok[0]), both(take_y, x_ok[1]), rng=X - 1, ang=Y + dy)
        plan(TAB.at[1 - side, pl.ds(0, SHARED), :], TABH.at[side], 8 + side, send_y, take_y, ang=Y + dy)
    sends = []
    takes = []

    def plan_send(src, dst, slot, send_if, **where):
        sends.append((send_if, pltpu.make_async_remote_copy(
            src_ref=src, dst_ref=dst, send_sem=ssem.at[count[0]], recv_sem=rsem.at[slot],
            device_id=where, device_id_type=MESH)))
        count[0] += 1

    def plan_take(dst, slot, take_if):
        takes.append((take_if, pltpu.make_async_remote_copy(
            src_ref=dst, dst_ref=dst, send_sem=ssem.at[0], recv_sem=rsem.at[slot],
            device_id=dict(aper=(A + 1) % 32), device_id_type=MESH)))

    for e in range(2):
        plan_send(PS.at[0, e], PB0.at[c0], 22 + c0, c0 != e, aper=4 * (2 * (top // 2) + e) + low)
        plan_take(PB0.at[e], 22 + e, c0 != e)
        for side in range(2):
            plan_send(PS.at[0, e, 1 - side], PB0H.at[side, c0], 32 + 2 * side + c0, y_ok[1 - side],
                      aper=4 * (2 * (top // 2) + e) + low, ang=Y + 1 - 2 * side)
            plan_take(PB0H.at[side, e], 32 + 2 * side + e, y_ok[side])
    for q in range(4):
        plan_send(PS.at[1, q // 2], PB1.at[t10], 18 + t10, t10 != q, aper=4 * (t2 * 4 + q) + low)
        plan_take(PB1.at[q], 18 + q, t10 != q)
        for side in range(2):
            plan_send(PS.at[1, q // 2, 1 - side], PB1H.at[side, t10], 24 + 4 * side + t10, y_ok[1 - side],
                      aper=4 * (t2 * 4 + q) + low, ang=Y + 1 - 2 * side)
            plan_take(PB1H.at[side, q], 24 + 4 * side + q, y_ok[side])
    for t in range(8):
        plan_send(PS.at[2, t // 4], PB2.at[top], 10 + top, top != t, aper=4 * t + low)
        plan_take(PB2.at[t], 10 + t, top != t)

    pl.semaphore_wait(barrier, 31 + 4 * ny + nx + nx * ny)
    for send_if, _, copy in copies:
        pl.when(send_if)(copy.start)
    for send_if, copy in sends:
        pl.when(send_if)(copy.start)

    k_at = row_of((256, 128))
    near = (jnp.where(k_at < 192, k_at, k_at - 256) - lane_of((256, 128))).astype(F32)
    for lvl in range(3):
        r0 = 16 * lvl
        for b in range(2):
            for h in range(2):
                lag = near - TAB[b, r0 + h:r0 + h + 1, :]
                taps = [TAB[b, r0 + 8 + 4 * h + t:r0 + 9 + 4 * h + t, :] for t in range(4)]
                RHS[lvl, b, :, 128 * h:128 * h + 128] = tap_matrix(lag, taps).astype(BF16)
                rows = shift_rows(TAB[b, r0 + 2 + h:r0 + 3 + h, :], TAB[b, r0 + 4 + h:r0 + 5 + h, :])
                for k, row in enumerate(rows):
                    WT[lvl, h, b, k:k + 1, :] = row

    def ramp_of(first, lvl):
        at = X * 128 - ROWS_BELOW_OUT[lvl] + first + row_of((16, 128))
        inside = jnp.logical_and(at >= 0, at < 512)
        return at.astype(F32) * (1.0 / 512) - 0.5, inside

    def swing(i, carry):
        first = pl.multiple_of(i * 16, 16)
        for lvl in range(3):
            ramp, inside = ramp_of(first, lvl)
            for b in range(2):
                cs = cos_sin(ramp * TAB[b, 16 * lvl + 6:16 * lvl + 7, :])
                for k in range(2):
                    EM[lvl, b, k, pl.ds(first, 16), :] = jnp.where(inside, cs[k], 0.0)
        return carry

    lax.fori_loop(0, 9, swing, 0)

    for _, take_if, copy in copies:
        pl.when(take_if)(copy.wait_recv)
    for take_if, copy in takes:
        pl.when(take_if)(copy.wait_recv)

    for h0 in range(2):
        for b in range(2):
            cs = cos_sin(PB0[h0, b])
            PC0[h0, b, 0], PC0[h0, b, 1] = cs
    for q in range(4):
        for b in range(2):
            cs = cos_sin(PB1[q, b])
            PC1[q, b, 0], PC1[q, b, 1] = cs
    for t in range(8):
        group = fp[16 * t:16 * t + 16, :]
        mine = group[0:4]
        for k in range(1, 4):
            mine = jnp.where(low == k, group[4 * k:4 * k + 4], mine)
        for b in range(2):
            cs = cos_sin(PB2[t, b] + mine[:, 128 * b:128 * b + 128])
            PC2[t, b, 0], PC2[t, b, 1] = cs

    lane1 = lane_of((1, 128))
    k_q = jnp.where(k_at < 64, 256 + k_at, jnp.where(k_at < 192, k_at - 128, k_at))

    def packed(lo, hi, width):
        half = width // 2
        lane = lane_of(lo.shape)
        got = jnp.where(lane < half, pltpu.roll(lo, half, 1), pltpu.roll(hi, half, 1))
        got = jnp.where(lane < width, got, 0.0)
        step = width
        while step < 128:
            got = got + pltpu.roll(got, step, 1)
            step *= 2
        return got

    for lvl in range(2):
        width = 16 >> lvl
        half = width // 2
        r0 = 16 * lvl
        tab = packed(TABH[0, r0:r0 + 16, :], TABH[1, r0:r0 + 16, :], width)

        def pick(first, second):
            return jnp.where(lane1 < 64, tab[first:first + 1], tab[second:second + 1])

        within = lane1 % width
        beam = jnp.where(within < half, within - half, 256 + within - half)
        lag = (k_q - beam).astype(F32) - pick(0, 1)
        full = tap_matrix(lag, [pick(8 + t, 12 + t) for t in range(4)])
        source = (lane1 // width) % (4 << lvl)
        dest = RHSH0 if lvl == 0 else RHSH1
        for m in range(4 << lvl):
            dest[m] = jnp.where(source == m, full, 0.0).astype(BF16)
        for k, row in enumerate(shift_rows(pick(2, 3), pick(4, 5))):
            WTH[lvl, k:k + 1, :] = row
        known = jnp.where(within < half, one(y_ok[0]), one(y_ok[1])) > 0

        def swing_halo(i, carry, lvl=lvl, rate=tab[6:7], known=known):
            first = pl.multiple_of(i * 16, 16)
            ramp, inside = ramp_of(first, lvl)
            cs = cos_sin(ramp * rate)
            ok = jnp.logical_and(inside, known)
            for k in range(2):
                EH[lvl, k, pl.ds(first, 16), :] = jnp.where(ok, cs[k], 0.0)
            return carry

        lax.fori_loop(0, 9, swing_halo, 0)
        owner = lane1 // width
        total = jnp.zeros((1, 128), F32)
        for q in range(2 << lvl):
            lo, hi = (PB0H[0, q], PB0H[1, q]) if lvl == 0 else (PB1H[0, q], PB1H[1, q])
            rows = packed(lo, hi, width)
            mine = 4 * q + row_of((4, 128)) == owner
            total = total + jnp.sum(jnp.where(mine, rows, 0.0), axis=0, keepdims=True)
        cs = cos_sin(total)
        for k in range(2):
            PCH[lvl, k, 0:1, :] = cs[k]

    left_half = lane_of((16, 128)) < 64

    def lay(dest, m, row, main0, main1, halo, beyond):
        dest[m, 0, pl.ds(row, 16), 0:128] = main0
        dest[m, 0, pl.ds(row, 16), 128:256] = jnp.where(left_half, main1, halo)
        dest[m, 1, pl.ds(row, 16), 0:128] = main1
        dest[m, 1, pl.ds(row, 16), 128:256] = jnp.where(left_half, halo, main0)
        if beyond:
            dest[m, 2, pl.ds(row, 16), 0:128] = halo
            dest[m, 2, pl.ds(row, 16), 128:256] = jnp.where(left_half, main0, main1)

    for j in range(4):
        for ri in range(2):
            img = 2 * j + ri
            for first in range(0, 160, 16):
                lo = pltpu.roll(PH[0, first:first + 16, :].astype(F32), (128 - 16 * img - 16) % 128, 1)
                hi = pltpu.roll(PH[1, first:first + 16, :].astype(F32), (128 - 16 * img) % 128, 1)
                halo = jnp.where(left_half, hi, lo).astype(BF16)
                lay(L0, j, 160 * ri + first, XM[img, 0, first:first + 16, :], XM[img, 1, first:first + 16, :], halo, True)

    def settle(src, at, dst, to, b4, b2, lvl, rows):
        d = ROWS_BELOW_IN[lvl] - ROWS_BELOW_OUT[lvl]
        for first in range(0, rows, 8):
            a, b, c, e = (src[at + (pl.ds(first + d + o, 8), slice(None))] for o in (-4, -2, 0, 2))
            dst[to + (pl.ds(first, 8), slice(None))] = jnp.where(b2, jnp.where(b4, e, b), jnp.where(b4, c, a))

    def three(src, at, first, w):
        return (
            w[0] * src[at + (pl.ds(first, 16), slice(None))]
            + w[1] * src[at + (pl.ds(first + 1, 16), slice(None))]
            + w[2] * src[at + (pl.ds(first + 2, 16), slice(None))]
        )

    def turn(re, im, c, s):
        return re * c - im * s, re * s + im * c

    for lvl in range(2):
        src, dst, tail = (L0, L1, RHSH0) if lvl == 0 else (L1, L2, RHSH1)
        rows = ROWS_IN[lvl]
        images = 4 << lvl
        width = 16 >> lvl
        phases = PC0 if lvl == 0 else PC1

        got = dot(src[0, 2], tail[0])
        for m in range(1, images):
            got = got + dot(src[m, 2], tail[m])
        for ri in range(2):
            IH[ri, 0:rows, :] = got[rows * ri:rows * ri + rows]
            settle(IH, (ri,), S2H, (ri,), WTH[lvl, 0:1, :] > 0.5, WTH[lvl, 1:2, :] > 0.5, lvl, 152)
        w = [WTH[lvl, k:k + 1, :] for k in (2, 3, 4)]
        for first in range(0, 144, 16):
            re, im = three(S2H, (0,), first, w), three(S2H, (1,), first, w)
            re, im = turn(re, im, EH[lvl, 0, first:first + 16, :], EH[lvl, 1, first:first + 16, :])
            re, im = turn(re, im, PCH[lvl, 0, 0:1, :], PCH[lvl, 1, 0:1, :])
            HB[0, first:first + 16, :] = re
            HB[1, first:first + 16, :] = im

        def image(m, carry, lvl=lvl, src=src, dst=dst, rows=rows, images=images, width=width, phases=phases):
            q = m // 4
            j = m % 4
            for b in range(2):
                got = dot(src[m, b], RHS[lvl, b])
                for h in range(2):
                    for ri in range(2):
                        IB[b, h, ri, 0:rows, :] = got[rows * ri:rows * ri + rows, 128 * h:128 * h + 128]
            for h in range(2):
                idx = images * h + m
                for b in range(2):
                    b4 = WT[lvl, h, b, 0:1, :] > 0.5
                    b2 = WT[lvl, h, b, 1:2, :] > 0.5
                    for ri in range(2):
                        settle(IB, (b, h, ri), S2, (h, b, ri), b4, b2, lvl, 152)
                w = [[WT[lvl, h, b, k:k + 1, :] for k in (2, 3, 4)] for b in range(2)]
                who = h if lvl == 0 else 2 * h + q
                turned = [[phases[who, b, k, pl.ds(j, 1), :] for k in range(2)] for b in range(2)]
                back = 128 - (width * idx + width // 2)
                for first in range(0, 144, 16):
                    main = []
                    for b in range(2):
                        re, im = three(S2, (h, b, 0), first, w[b]), three(S2, (h, b, 1), first, w[b])
                        re, im = turn(re, im, EM[lvl, b, 0, first:first + 16, :], EM[lvl, b, 1, first:first + 16, :])
                        main.append(turn(re, im, turned[b][0], turned[b][1]))
                    for ri in range(2):
                        halo = pltpu.roll(HB[ri, first:first + 16, :], back, 1).astype(BF16)
                        lay(dst, idx, 144 * ri + first, main[0][ri].astype(BF16), main[1][ri].astype(BF16), halo, lvl == 0)
            return carry

        lax.fori_loop(0, images, image, 0)

    def rs_copy(k):
        return pltpu.make_async_remote_copy(
            src_ref=SB.at[k], dst_ref=RS.at[A], send_sem=rs_ssem.at[k], recv_sem=rs_rsem.at[A],
            device_id=dict(aper=k), device_id_type=MESH)

    for b in range(2):
        ACC[...] = jnp.zeros((2, 2, 144, 128), F32)

        def gather(n, carry, b=b):
            got = dot(L2[n, b], RHS[2, b])
            for h in range(2):
                t = 4 * h + n // 4
                c = PC2[t, b, 0, pl.ds(n % 4, 1), :]
                s = PC2[t, b, 1, pl.ds(n % 4, 1), :]
                for first in range(0, 136, 8):
                    re = got[first:first + 8, 128 * h:128 * h + 128]
                    im = got[144 + first:152 + first, 128 * h:128 * h + 128]
                    re, im = turn(re, im, c, s)
                    ACC[h, 0, first:first + 8, :] += re
                    ACC[h, 1, first:first + 8, :] += im
            return carry

        lax.fori_loop(0, 16, gather, 0)
        for h in range(2):
            b4 = WT[2, h, b, 0:1, :] > 0.5
            b2 = WT[2, h, b, 1:2, :] > 0.5
            for ri in range(2):
                settle(ACC, (h, ri), S2, (h, b, ri), b4, b2, 2, 136)
        w = [[WT[2, h, b, k:k + 1, :] for k in (2, 3, 4)] for h in range(2)]
        for first in range(0, 128, 16):
            re = three(S2, (0, b, 0), first, w[0]) + three(S2, (1, b, 0), first, w[1])
            im = three(S2, (0, b, 1), first, w[0]) + three(S2, (1, b, 1), first, w[1])
            re, im = turn(re, im, EM[2, b, 0, first:first + 16, :], EM[2, b, 1, first:first + 16, :])
            FB[0, first:first + 16, :] = re.astype(BF16)
            FB[1, first:first + 16, :] = im.astype(BF16)
        parts = [lax.dot_general(eye, FB[ri], NT, preferred_element_type=F32).reshape(16, 8, 128) for ri in range(2)]
        SB[16 * b:16 * b + 16] = jnp.concatenate(parts, axis=1).astype(BF16)

        def send(k, carry):
            @pl.when(k != A)
            def _():
                rs_copy(k).start()
            return carry

        lax.fori_loop(16 * b, 16 * b + 16, send, 0)

    RS[A] = SB[A]

    def arrive(k, total):
        @pl.when(k != A)
        def _():
            pltpu.make_async_remote_copy(
                src_ref=SB.at[k], dst_ref=RS.at[k], send_sem=rs_ssem.at[k], recv_sem=rs_rsem.at[k],
                device_id=dict(aper=k), device_id_type=MESH).wait_recv()
        return total + RS[k].astype(F32)

    total = lax.fori_loop(0, 32, arrive, jnp.zeros((16, 128), F32)) * (1.0 / math.sqrt(128.0))
    out[0, 0] = total[0:8]
    out[1, 0] = total[8:16]

    for send_if, _, copy in copies:
        pl.when(send_if)(copy.wait_send)
    for send_if, copy in sends:
        pl.when(send_if)(copy.wait_send)

    def sent(k, carry):
        @pl.when(k != A)
        def _():
            rs_copy(k).wait_send()
        return carry

    lax.fori_loop(0, 32, sent, 0)


def body(*args):
    v = pltpu.VMEM
    return pl.pallas_call(
        kernel,
        out_shape=jax.ShapeDtypeStruct((2, 1, 8, 128), F32),
        in_specs=[pl.BlockSpec(memory_space=pltpu.VMEM)] * 8,
        out_specs=pl.BlockSpec(memory_space=pltpu.VMEM),
        scratch_shapes=[
            v((8, 2, 160, 128), BF16),
            v((2, 128, 128), BF16),
            v((2, 160, 128), BF16),
            v((2, 48, 128), F32),
            v((2, 32, 128), F32),
            v((3, 2, 2, 4, 128), F32),
            v((8, 2, 4, 128), F32),
            v((4, 2, 4, 128), F32),
            v((2, 2, 4, 128), F32),
            v((2, 4, 4, 128), F32),
            v((2, 2, 4, 128), F32),
            v((3, 2, 256, 256), BF16),
            v((4, 256, 128), BF16),
            v((8, 256, 128), BF16),
            v((3, 2, 2, 8, 128), F32),
            v((2, 8, 128), F32),
            v((3, 2, 2, 144, 128), F32),
            v((2, 2, 144, 128), F32),
            v((8, 2, 2, 4, 128), F32),
            v((4, 2, 2, 4, 128), F32),
            v((2, 2, 2, 4, 128), F32),
            v((2, 2, 8, 128), F32),
            v((4, 3, 320, 256), BF16),
            v((8, 3, 288, 256), BF16),
            v((16, 2, 288, 256), BF16),
            v((2, 2, 2, 176, 128), F32),
            v((2, 176, 128), F32),
            v((2, 2, 2, 160, 128), F32),
            v((2, 160, 128), F32),
            v((2, 144, 128), F32),
            v((2, 2, 144, 128), F32),
            v((2, 128, 128), BF16),
            v((32, 16, 128), BF16),
            v((32, 16, 128), BF16),
            pltpu.SemaphoreType.DMA((48,)),
            pltpu.SemaphoreType.DMA((48,)),
            pltpu.SemaphoreType.DMA((32,)),
            pltpu.SemaphoreType.DMA((32,)),
        ],
        compiler_params=pltpu.CompilerParams(collective_id=0, has_side_effects=True, vmem_limit_bytes=48 * 1024 * 1024),
    )(*args)


def solution(mesh):
    in_specs = (
        P("aper", None, "ang", "rng"),
        P(None, None, None, "ang"),
        P(None, None, None, "ang"),
        P(None, None, None, None, "ang"),
        P(None, None, None, "ang"),
        P("aper", None, None, "ang"),
        P(None, None, "ang"),
        P(None, "ang"),
    )
    out_specs = P(None, "ang", "aper", "rng")
    return jax.shard_map(body, mesh=mesh, in_specs=in_specs, out_specs=out_specs, check_vma=False)
```

profile of v0, /device:TPU:61, one launch (start us, length us, event | category | flops | bytes accessed | tf_op | source)
XLA Modules:
  0.0 53.9 jit_solution(6151872226297864350)
XLA Ops:
  0.0 0.0 copy-start
  0.0 1.0 %copy-done = bf16[4,2,256,128]{3,2,1,0:T(8,128)(2,1)S(1)} copy-done((bf16[4,2,256,128]{3,2,1,0:T(8,128)(2,1)S(1)}, bf16[4,2,256,128]{3,2,1,0:T(8,128)(2,1)}, u32[]{:S(2)}) %copy-start) | copy-done | bytes 524312
  1.0 0.0 copy-start.1
  1.0 0.9 %copy-done.1 = f32[128,256]{1,0:T(8,128)S(1)} copy-done((f32[128,256]{1,0:T(8,128)S(1)}, f32[128,256]{1,0:T(8,128)}, u32[]{:S(2)}) %copy-start.1) | copy-done | bytes 131096
  1.9 0.0 copy-start.2
  1.9 0.7 %copy-done.2 = bf16[3,2,2,4,256]{4,3,2,1,0:T(4,128)(2,1)S(1)} copy-done((bf16[3,2,2,4,256]{4,3,2,1,0:T(4,128)(2,1)S(1)}, bf16[3,2,2,4,256]{4,3,2,1,0:T(4,128)(2,1)}, u32[]{:S(2)}) %copy-start.2) | copy-done | bytes 24600
  2.7 0.0 copy-start.3
  2.7 0.7 %copy-done.3 = f32[4,3,2,256]{3,2,1,0:T(2,128)S(1)} copy-done((f32[4,3,2,256]{3,2,1,0:T(2,128)S(1)}, f32[4,3,2,256]{3,2,1,0:T(2,128)}, u32[]{:S(2)}) %copy-start.3) | copy-done | bytes 24600
  3.4 0.0 copy-start.4
  3.4 0.7 %copy-done.4 = s32[3,2,2,256]{3,2,1,0:T(2,128)S(1)} copy-done((s32[3,2,2,256]{3,2,1,0:T(2,128)S(1)}, s32[3,2,2,256]{3,2,1,0:T(2,128)}, u32[]{:S(2)}) %copy-start.4) | copy-done | bytes 12312
  4.1 0.0 copy-start.5
  4.1 0.7 %copy-done.5 = s32[3,2,2,256]{3,2,1,0:T(2,128)S(1)} copy-done((s32[3,2,2,256]{3,2,1,0:T(2,128)S(1)}, s32[3,2,2,256]{3,2,1,0:T(2,128)}, u32[]{:S(2)}) %copy-start.5) | copy-done | bytes 12312
  4.8 0.0 copy-start.6
  4.8 0.7 %copy-done.6 = f32[3,2,2,256]{3,2,1,0:T(2,128)S(1)} copy-done((f32[3,2,2,256]{3,2,1,0:T(2,128)S(1)}, f32[3,2,2,256]{3,2,1,0:T(2,128)}, u32[]{:S(2)}) %copy-start.6) | copy-done | bytes 12312
  5.5 0.0 copy-start.7
  5.5 0.7 %copy-done.7 = f32[3,2,256]{2,1,0:T(2,128)S(1)} copy-done((f32[3,2,256]{2,1,0:T(2,128)S(1)}, f32[3,2,256]{2,1,0:T(2,128)}, u32[]{:S(2)}) %copy-start.7) | copy-done | bytes 6168
  6.2 47.1 %shard_map.82 = f32[2,1,8,128]{3,2,1,0:T(8,128)S(1)} custom-call(bf16[4,2,256,128]{3,2,1,0:T(8,128)(2,1)S(1)} %copy-done, s32[3,2,2,256]{3,2,1,0:T(2,128)S(1)} %copy-done.4, s32[3,2,2,256]{3,2,1,0:T(2,128)S(1)} %copy-done.5, bf16[3,2,2,4,256]{4,3,2,1,0:T(4,128)(2,1)S(1)} %copy-done.2, f32[3,2,2,256]{3,2,1,0:T(2,128)S(1)} %copy-done.6, ...), custom_call_target="tpu_custom_call" | custom-call | tf_op jit(solution)/shard_map/pallas_call | solution.py:511
  53.3 0.6 %copy.10 = f32[2,1,8,128]{3,2,1,0:T(8,128)} copy(f32[2,1,8,128]{3,2,1,0:T(8,128)S(1)} %shard_map.82) | data formatting | bytes 16384
Async XLA Ops:
  0.0 1.0 %copy-start = (bf16[4,2,256,128]{3,2,1,0:T(8,128)(2,1)S(1)}, bf16[4,2,256,128]{3,2,1,0:T(8,128)(2,1)}, u32[]{:S(2)}) copy-start(bf16[4,2,256,128]{3,2,1,0:T(8,128)(2,1)} %sub.1) | copy-start | bytes 1572868
  1.0 0.9 %copy-start.1 = (f32[128,256]{1,0:T(8,128)S(1)}, f32[128,256]{1,0:T(8,128)}, u32[]{:S(2)}) copy-start(f32[128,256]{1,0:T(8,128)} %fp.1) | copy-start | bytes 393220
  1.9 0.7 %copy-start.2 = (bf16[3,2,2,4,256]{4,3,2,1,0:T(4,128)(2,1)S(1)}, bf16[3,2,2,4,256]{4,3,2,1,0:T(4,128)(2,1)}, u32[]{:S(2)}) copy-start(bf16[3,2,2,4,256]{4,3,2,1,0:T(4,128)(2,1)} %bt.1) | copy-start | bytes 73732
  2.7 0.7 %copy-start.3 = (f32[4,3,2,256]{3,2,1,0:T(2,128)S(1)}, f32[4,3,2,256]{3,2,1,0:T(2,128)}, u32[]{:S(2)}) copy-start(f32[4,3,2,256]{3,2,1,0:T(2,128)} %pb.1) | copy-start | bytes 73732
  3.4 0.7 %copy-start.4 = (s32[3,2,2,256]{3,2,1,0:T(2,128)S(1)}, s32[3,2,2,256]{3,2,1,0:T(2,128)}, u32[]{:S(2)}) copy-start(s32[3,2,2,256]{3,2,1,0:T(2,128)} %bo.1) | copy-start | bytes 36868
  4.1 0.7 %copy-start.5 = (s32[3,2,2,256]{3,2,1,0:T(2,128)S(1)}, s32[3,2,2,256]{3,2,1,0:T(2,128)}, u32[]{:S(2)}) copy-start(s32[3,2,2,256]{3,2,1,0:T(2,128)} %ro.1) | copy-start | bytes 36868
  4.8 0.7 %copy-start.6 = (f32[3,2,2,256]{3,2,1,0:T(2,128)S(1)}, f32[3,2,2,256]{3,2,1,0:T(2,128)}, u32[]{:S(2)}) copy-start(f32[3,2,2,256]{3,2,1,0:T(2,128)} %rf.1) | copy-start | bytes 36868
  5.5 0.7 %copy-start.7 = (f32[3,2,256]{2,1,0:T(2,128)S(1)}, f32[3,2,256]{2,1,0:T(2,128)}, u32[]{:S(2)}) copy-start(f32[3,2,256]{2,1,0:T(2,128)} %pr.1) | copy-start | bytes 18436
where the time goes:
time: 54.4 us; the launch traced here: 53.9 us
  Pallas kernels  47.1 us (87%)
  local copies, waits for them, and re-layouts  6.83 us (13%)
    pallas_call x1, Pallas kernels, body(): pl.pallas_call(kernel, out_shape=jax.ShapeDtypeStruct((2, 1, 8, 128), F32...  47.1 us
    unnamed x17, local copies, waits for them, and re-layouts  6.83 us

commit v1 on v0

--- a/solution.py
+++ b/solution.py
@@ -67,12 +67,22 @@
 
 
 def kernel(
-    sub, bo, ro, bt, rf, pb, pr, fp, out,
-    XM, PE, PH, TAB, TABH, PS, PB2, PB1, PB0, PB1H, PB0H,
+    *refs,
+):
+    ins, rest = refs[:8], refs[8:]
+    out = rest[0]
+    here = rest[1:9]
+    in_sem = rest[9]
+    (sub, bo, ro, bt, rf, pb, pr, fp) = here
+    (
+    XS, XR, PE, PH, TAB, TABH, PS, PB2, PB1, PB0, PB1H, PB0H,
     RHS, RHSH0, RHSH1, WT, WTH, EM, EH, PC2, PC1, PC0, PCH,
     L0, L1, L2, IB, IH, S2, S2H, HB, ACC, FB, SB, RS,
     ssem, rsem, rs_ssem, rs_rsem,
-):
+    ) = rest[10:]
+    loads = [pltpu.make_async_copy(ins[k], here[k], in_sem.at[k]) for k in (5, 0, 1, 2, 3, 4, 6, 7)]
+    for load in loads:
+        load.start()
     A = lax.axis_index("aper")
     X = lax.axis_index("rng")
     Y = lax.axis_index("ang")
@@ -114,12 +124,18 @@
     ny = one(y_ok[0]) + one(y_ok[1])
     nx = one(x_ok[0]) + one(x_ok[1])
 
+    for load in loads:
+        load.wait()
+
     eye = jnp.where(row_of((128, 128)) == lane_of((128, 128)), 1.0, 0.0).astype(BF16)
     for j in range(4):
         for ri in range(2):
             turned = lax.dot_general(eye, sub[j, ri], NT, preferred_element_type=F32).astype(BF16)
-            XM[2 * j + ri, 0, 16:144, :] = turned[:, 0:128]
-            XM[2 * j + ri, 1, 16:144, :] = turned[:, 128:256]
+            for b in range(2):
+                main = turned[:, 128 * b:128 * b + 128]
+                L0[b, 320 * j + 160 * ri + 16:320 * j + 160 * ri + 144, 0:128] = main
+                XS[2 * j + ri, b, 0] = main[0:16]
+                XS[2 * j + ri, b, 1] = main[112:128]
     for side, first in ((0, 0), (1, 240)):
         edge = sub[:, :, first:first + 16, :].reshape(128, 128)
         PE[side] = lax.dot_general(eye, edge, NT, preferred_element_type=F32).astype(BF16)
@@ -155,12 +171,12 @@
 
     @pl.when(X == 0)
     def _():
-        XM[:, :, 0:16, :] = jnp.zeros((8, 2, 16, 128), BF16)
+        XR[:, :, 0] = jnp.zeros((8, 2, 16, 128), BF16)
         PH[:, 0:16, :] = jnp.zeros((2, 16, 128), BF16)
 
     @pl.when(X == 3)
     def _():
-        XM[:, :, 144:160, :] = jnp.zeros((8, 2, 16, 128), BF16)
+        XR[:, :, 1] = jnp.zeros((8, 2, 16, 128), BF16)
         PH[:, 144:160, :] = jnp.zeros((2, 16, 128), BF16)
 
     for side, edge_at in ((0, 0), (1, 3)):
@@ -170,6 +186,36 @@
             TABH[side] = jnp.zeros((SHARED, 128), F32)
             PB1H[side] = jnp.zeros((4, 4, 128), F32)
             PB0H[side] = jnp.zeros((2, 4, 128), F32)
+
+    k_at = row_of((256, 128))
+    near = (jnp.where(k_at < 192, k_at, k_at - 256) - lane_of((256, 128))).astype(F32)
+    for lvl in range(3):
+        r0 = 16 * lvl
+        for b in range(2):
+            for h in range(2):
+                lag = near - TAB[b, r0 + h:r0 + h + 1, :]
+                taps = [TAB[b, r0 + 8 + 4 * h + t:r0 + 9 + 4 * h + t, :] for t in range(4)]
+                RHS[lvl, b, :, 128 * h:128 * h + 128] = tap_matrix(lag, taps).astype(BF16)
+                rows = shift_rows(TAB[b, r0 + 2 + h:r0 + 3 + h, :], TAB[b, r0 + 4 + h:r0 + 5 + h, :])
+                for k, row in enumerate(rows):
+                    WT[lvl, h, b, k:k + 1, :] = row
+
+    def ramp_of(first, lvl):
+        at = X * 128 - ROWS_BELOW_OUT[lvl] + first + row_of((16, 128))
+        inside = jnp.logical_and(at >= 0, at < 512)
+        return at.astype(F32) * (1.0 / 512) - 0.5, inside
+
+    def swing(i, carry):
+        first = pl.multiple_of(i * 16, 16)
+        for lvl in range(3):
+            ramp, inside = ramp_of(first, lvl)
+            for b in range(2):
+                cs = cos_sin(ramp * TAB[b, 16 * lvl + 6:16 * lvl + 7, :])
+                for k in range(2):
+                    EM[lvl, b, k, pl.ds(first, 16), :] = jnp.where(inside, cs[k], 0.0)
+        return carry
+
+    lax.fori_loop(0, 9, swing, 0)
 
     copies = []
     count = [0]
@@ -184,8 +230,8 @@
         ))
         count[0] += 1
 
-    plan(XM.at[:, :, pl.ds(128, 16), :], XM.at[:, :, pl.ds(0, 16), :], 0, x_ok[1], x_ok[0], rng=X + 1)
-    plan(XM.at[:, :, pl.ds(16, 16), :], XM.at[:, :, pl.ds(144, 16), :], 1, x_ok[0], x_ok[1], rng=X - 1)
+    plan(XS.at[:, :, 1], XR.at[:, :, 0], 0, x_ok[1], x_ok[0], rng=X + 1)
+    plan(XS.at[:, :, 0], XR.at[:, :, 1], 1, x_ok[0], x_ok[1], rng=X - 1)
     both = jnp.logical_and
     for side in range(2):
         dy = 1 - 2 * side
@@ -198,7 +244,7 @@
              both(send_y, x_ok[0]), both(take_y, x_ok[1]), rng=X - 1, ang=Y + dy)
         plan(TAB.at[1 - side, pl.ds(0, SHARED), :], TABH.at[side], 8 + side, send_y, take_y, ang=Y + dy)
     sends = []
-    takes = []
+    takes = ([], [], [])
 
     def plan_send(src, dst, slot, send_if, **where):
         sends.append((send_if, pltpu.make_async_remote_copy(
@@ -206,28 +252,28 @@
             device_id=where, device_id_type=MESH)))
         count[0] += 1
 
-    def plan_take(dst, slot, take_if):
-        takes.append((take_if, pltpu.make_async_remote_copy(
+    def plan_take(lvl, dst, slot, take_if):
+        takes[lvl].append((take_if, pltpu.make_async_remote_copy(
             src_ref=dst, dst_ref=dst, send_sem=ssem.at[0], recv_sem=rsem.at[slot],
             device_id=dict(aper=(A + 1) % 32), device_id_type=MESH)))
 
     for e in range(2):
         plan_send(PS.at[0, e], PB0.at[c0], 22 + c0, c0 != e, aper=4 * (2 * (top // 2) + e) + low)
-        plan_take(PB0.at[e], 22 + e, c0 != e)
+        plan_take(0, PB0.at[e], 22 + e, c0 != e)
         for side in range(2):
             plan_send(PS.at[0, e, 1 - side], PB0H.at[side, c0], 32 + 2 * side + c0, y_ok[1 - side],
                       aper=4 * (2 * (top // 2) + e) + low, ang=Y + 1 - 2 * side)
-            plan_take(PB0H.at[side, e], 32 + 2 * side + e, y_ok[side])
+            plan_take(0, PB0H.at[side, e], 32 + 2 * side + e, y_ok[side])
     for q in range(4):
         plan_send(PS.at[1, q // 2], PB1.at[t10], 18 + t10, t10 != q, aper=4 * (t2 * 4 + q) + low)
-        plan_take(PB1.at[q], 18 + q, t10 != q)
+        plan_take(1, PB1.at[q], 18 + q, t10 != q)
         for side in range(2):
             plan_send(PS.at[1, q // 2, 1 - side], PB1H.at[side, t10], 24 + 4 * side + t10, y_ok[1 - side],
                       aper=4 * (t2 * 4 + q) + low, ang=Y + 1 - 2 * side)
-            plan_take(PB1H.at[side, q], 24 + 4 * side + q, y_ok[side])
+            plan_take(1, PB1H.at[side, q], 24 + 4 * side + q, y_ok[side])
     for t in range(8):
         plan_send(PS.at[2, t // 4], PB2.at[top], 10 + top, top != t, aper=4 * t + low)
-        plan_take(PB2.at[t], 10 + t, top != t)
+        plan_take(2, PB2.at[t], 10 + t, top != t)
 
     pl.semaphore_wait(barrier, 31 + 4 * ny + nx + nx * ny)
     for send_if, _, copy in copies:
@@ -235,57 +281,8 @@
     for send_if, copy in sends:
         pl.when(send_if)(copy.start)
 
-    k_at = row_of((256, 128))
-    near = (jnp.where(k_at < 192, k_at, k_at - 256) - lane_of((256, 128))).astype(F32)
-    for lvl in range(3):
-        r0 = 16 * lvl
-        for b in range(2):
-            for h in range(2):
-                lag = near - TAB[b, r0 + h:r0 + h + 1, :]
-                taps = [TAB[b, r0 + 8 + 4 * h + t:r0 + 9 + 4 * h + t, :] for t in range(4)]
-                RHS[lvl, b, :, 128 * h:128 * h + 128] = tap_matrix(lag, taps).astype(BF16)
-                rows = shift_rows(TAB[b, r0 + 2 + h:r0 + 3 + h, :], TAB[b, r0 + 4 + h:r0 + 5 + h, :])
-                for k, row in enumerate(rows):
-                    WT[lvl, h, b, k:k + 1, :] = row
-
-    def ramp_of(first, lvl):
-        at = X * 128 - ROWS_BELOW_OUT[lvl] + first + row_of((16, 128))
-        inside = jnp.logical_and(at >= 0, at < 512)
-        return at.astype(F32) * (1.0 / 512) - 0.5, inside
-
-    def swing(i, carry):
-        first = pl.multiple_of(i * 16, 16)
-        for lvl in range(3):
-            ramp, inside = ramp_of(first, lvl)
-            for b in range(2):
-                cs = cos_sin(ramp * TAB[b, 16 * lvl + 6:16 * lvl + 7, :])
-                for k in range(2):
-                    EM[lvl, b, k, pl.ds(first, 16), :] = jnp.where(inside, cs[k], 0.0)
-        return carry
-
-    lax.fori_loop(0, 9, swing, 0)
-
     for _, take_if, copy in copies:
         pl.when(take_if)(copy.wait_recv)
-    for take_if, copy in takes:
-        pl.when(take_if)(copy.wait_recv)
-
-    for h0 in range(2):
-        for b in range(2):
-            cs = cos_sin(PB0[h0, b])
-            PC0[h0, b, 0], PC0[h0, b, 1] = cs
-    for q in range(4):
-        for b in range(2):
-            cs = cos_sin(PB1[q, b])
-            PC1[q, b, 0], PC1[q, b, 1] = cs
-    for t in range(8):
-        group = fp[16 * t:16 * t + 16, :]
-        mine = group[0:4]
-        for k in range(1, 4):
-            mine = jnp.where(low == k, group[4 * k:4 * k + 4], mine)
-        for b in range(2):
-            cs = cos_sin(PB2[t, b] + mine[:, 128 * b:128 * b + 128])
-            PC2[t, b, 0], PC2[t, b, 1] = cs
 
     lane1 = lane_of((1, 128))
     k_q = jnp.where(k_at < 64, 256 + k_at, jnp.where(k_at < 192, k_at - 128, k_at))
@@ -301,7 +298,7 @@
             step *= 2
         return got
 
-    for lvl in range(2):
+    def beyond_tables(lvl):
         width = 16 >> lvl
         half = width // 2
         r0 = 16 * lvl
@@ -332,6 +329,9 @@
             return carry
 
         lax.fori_loop(0, 9, swing_halo, 0)
+
+    def beyond_phases(lvl):
+        width = 16 >> lvl
         owner = lane1 // width
         total = jnp.zeros((1, 128), F32)
         for q in range(2 << lvl):
@@ -345,14 +345,16 @@
 
     left_half = lane_of((16, 128)) < 64
 
-    def lay(dest, m, row, main0, main1, halo, beyond):
-        dest[m, 0, pl.ds(row, 16), 0:128] = main0
-        dest[m, 0, pl.ds(row, 16), 128:256] = jnp.where(left_half, main1, halo)
-        dest[m, 1, pl.ds(row, 16), 0:128] = main1
-        dest[m, 1, pl.ds(row, 16), 128:256] = jnp.where(left_half, halo, main0)
+    def lay(dest, row, main0, main1, halo, beyond, main_too=True):
+        rows = pl.ds(row, 16)
+        if main_too:
+            dest[0, rows, 0:128] = main0
+            dest[1, rows, 0:128] = main1
+        dest[0, rows, 128:256] = jnp.where(left_half, main1, halo)
+        dest[1, rows, 128:256] = jnp.where(left_half, halo, main0)
         if beyond:
-            dest[m, 2, pl.ds(row, 16), 0:128] = halo
-            dest[m, 2, pl.ds(row, 16), 128:256] = jnp.where(left_half, main0, main1)
+            dest[2, rows, 0:128] = halo
+            dest[2, rows, 128:256] = jnp.where(left_half, main0, main1)
 
     for j in range(4):
         for ri in range(2):
@@ -361,7 +363,10 @@
                 lo = pltpu.roll(PH[0, first:first + 16, :].astype(F32), (128 - 16 * img - 16) % 128, 1)
                 hi = pltpu.roll(PH[1, first:first + 16, :].astype(F32), (128 - 16 * img) % 128, 1)
                 halo = jnp.where(left_half, hi, lo).astype(BF16)
-                lay(L0, j, 160 * ri + first, XM[img, 0, first:first + 16, :], XM[img, 1, first:first + 16, :], halo, True)
+                row = 320 * j + 160 * ri + first
+                edge = first in (0, 144)
+                main = [XR[img, b, first // 144] if edge else L0[b, row:row + 16, 0:128] for b in range(2)]
+                lay(L0, row, main[0], main[1], halo, True, edge)
 
     def settle(src, at, dst, to, b4, b2, lvl, rows):
         d = ROWS_BELOW_IN[lvl] - ROWS_BELOW_OUT[lvl]
@@ -386,9 +391,23 @@
         width = 16 >> lvl
         phases = PC0 if lvl == 0 else PC1
 
-        got = dot(src[0, 2], tail[0])
+        beyond_tables(lvl)
+        for take_if, copy in takes[lvl]:
+            pl.when(take_if)(copy.wait_recv)
+        beyond_phases(lvl)
+        if lvl == 0:
+            for h0 in range(2):
+                for b in range(2):
+                    cs = cos_sin(PB0[h0, b])
+                    PC0[h0, b, 0], PC0[h0, b, 1] = cs
+        else:
+            for q in range(4):
+                for b in range(2):
+                    cs = cos_sin(PB1[q, b])
+                    PC1[q, b, 0], PC1[q, b, 1] = cs
+        got = dot(src[2, 0:2 * rows, :], tail[0])
         for m in range(1, images):
-            got = got + dot(src[m, 2], tail[m])
+            got = got + dot(src[2, 2 * rows * m:2 * rows * m + 2 * rows, :], tail[m])
         for ri in range(2):
             IH[ri, 0:rows, :] = got[rows * ri:rows * ri + rows]
             settle(IH, (ri,), S2H, (ri,), WTH[lvl, 0:1, :] > 0.5, WTH[lvl, 1:2, :] > 0.5, lvl, 152)
@@ -400,37 +419,55 @@
             HB[0, first:first + 16, :] = re
             HB[1, first:first + 16, :] = im
 
-        def image(m, carry, lvl=lvl, src=src, dst=dst, rows=rows, images=images, width=width, phases=phases):
-            q = m // 4
-            j = m % 4
-            for b in range(2):
-                got = dot(src[m, b], RHS[lvl, b])
+        def two_images(i, carry, lvl=lvl, src=src, dst=dst, rows=rows, images=images, width=width, phases=phases):
+            for u in range(2):
+                at = pl.multiple_of((2 * i + u) * (2 * rows), 2 * rows)
+                for b in range(2):
+                    got = dot(src[b, pl.ds(at, 2 * rows), :], RHS[lvl, b])
+                    for h in range(2):
+                        for ri in range(2):
+                            IB[u, b, h, ri, 0:rows, :] = got[rows * ri:rows * ri + rows, 128 * h:128 * h + 128]
+            for u in range(2):
+                m = 2 * i + u
+                q = m // 4
+                j = m % 4
+                w, turned, back = [], [], []
                 for h in range(2):
-                    for ri in range(2):
-                        IB[b, h, ri, 0:rows, :] = got[rows * ri:rows * ri + rows, 128 * h:128 * h + 128]
-            for h in range(2):
-                idx = images * h + m
-                for b in range(2):
-                    b4 = WT[lvl, h, b, 0:1, :] > 0.5
-                    b2 = WT[lvl, h, b, 1:2, :] > 0.5
-                    for ri in range(2):
-                        settle(IB, (b, h, ri), S2, (h, b, ri), b4, b2, lvl, 152)
-                w = [[WT[lvl, h, b, k:k + 1, :] for k in (2, 3, 4)] for b in range(2)]
-                who = h if lvl == 0 else 2 * h + q
-                turned = [[phases[who, b, k, pl.ds(j, 1), :] for k in range(2)] for b in range(2)]
-                back = 128 - (width * idx + width // 2)
+                    for b in range(2):
+                        b4 = WT[lvl, h, b, 0:1, :] > 0.5
+                        b2 = WT[lvl, h, b, 1:2, :] > 0.5
+                        for ri in range(2):
+                            settle(IB, (u, b, h, ri), S2, (u, h, b, ri), b4, b2, lvl, 152)
+                    w.append([[WT[lvl, h, b, k:k + 1, :] for k in (2, 3, 4)] for b in range(2)])
+                    who = h if lvl == 0 else 2 * h + q
+                    turned.append([[phases[who, b, k, pl.ds(j, 1), :] for k in range(2)] for b in range(2)])
+                    back.append(128 - (width * (images * h + m) + width // 2))
                 for first in range(0, 144, 16):
-                    main = []
-                    for b in range(2):
-                        re, im = three(S2, (h, b, 0), first, w[b]), three(S2, (h, b, 1), first, w[b])
-                        re, im = turn(re, im, EM[lvl, b, 0, first:first + 16, :], EM[lvl, b, 1, first:first + 16, :])
-                        main.append(turn(re, im, turned[b][0], turned[b][1]))
-                    for ri in range(2):
-                        halo = pltpu.roll(HB[ri, first:first + 16, :], back, 1).astype(BF16)
-                        lay(dst, idx, 144 * ri + first, main[0][ri].astype(BF16), main[1][ri].astype(BF16), halo, lvl == 0)
+                    swings = [[EM[lvl, b, k, first:first + 16, :] for k in range(2)] for b in range(2)]
+                    for h in range(2):
+                        main = []
+                        for b in range(2):
+                            re, im = three(S2, (u, h, b, 0), first, w[h][b]), three(S2, (u, h, b, 1), first, w[h][b])
+                            re, im = turn(re, im, swings[b][0], swings[b][1])
+                            main.append(turn(re, im, turned[h][b][0], turned[h][b][1]))
+                        for ri in range(2):
+                            halo = pltpu.roll(HB[ri, first:first + 16, :], back[h], 1).astype(BF16)
+                            row = pl.multiple_of((images * h + m) * 288 + 144 * ri + first, 16)
+                            lay(dst, row, main[0][ri].astype(BF16), main[1][ri].astype(BF16), halo, lvl == 0)
             return carry
 
-        lax.fori_loop(0, images, image, 0)
+        lax.fori_loop(0, images // 2, two_images, 0)
+
+    for take_if, copy in takes[2]:
+        pl.when(take_if)(copy.wait_recv)
+    for t in range(8):
+        group = fp[16 * t:16 * t + 16, :]
+        mine = group[0:4]
+        for k in range(1, 4):
+            mine = jnp.where(low == k, group[4 * k:4 * k + 4], mine)
+        for b in range(2):
+            cs = cos_sin(PB2[t, b] + mine[:, 128 * b:128 * b + 128])
+            PC2[t, b, 0], PC2[t, b, 1] = cs
 
     def rs_copy(k):
         return pltpu.make_async_remote_copy(
@@ -440,30 +477,34 @@
     for b in range(2):
         ACC[...] = jnp.zeros((2, 2, 144, 128), F32)
 
-        def gather(n, carry, b=b):
-            got = dot(L2[n, b], RHS[2, b])
+        def gather(i, carry, b=b):
+            at = pl.multiple_of(i * 1152, 1152)
+            got = dot(L2[b, pl.ds(at, 1152), :], RHS[2, b])
             for h in range(2):
-                t = 4 * h + n // 4
-                c = PC2[t, b, 0, pl.ds(n % 4, 1), :]
-                s = PC2[t, b, 1, pl.ds(n % 4, 1), :]
+                c = [PC2[4 * h + i, b, 0, j:j + 1, :] for j in range(4)]
+                s = [PC2[4 * h + i, b, 1, j:j + 1, :] for j in range(4)]
                 for first in range(0, 136, 8):
-                    re = got[first:first + 8, 128 * h:128 * h + 128]
-                    im = got[144 + first:152 + first, 128 * h:128 * h + 128]
-                    re, im = turn(re, im, c, s)
-                    ACC[h, 0, first:first + 8, :] += re
-                    ACC[h, 1, first:first + 8, :] += im
+                    re, im = ACC[h, 0, first:first + 8, :], ACC[h, 1, first:first + 8, :]
+                    for j in range(4):
+                        row = 288 * j + first
+                        x = got[row:row + 8, 128 * h:128 * h + 128]
+                        y = got[row + 144:row + 152, 128 * h:128 * h + 128]
+                        re = re + (x * c[j] - y * s[j])
+                        im = im + (x * s[j] + y * c[j])
+                    ACC[h, 0, first:first + 8, :] = re
+                    ACC[h, 1, first:first + 8, :] = im
             return carry
 
-        lax.fori_loop(0, 16, gather, 0)
+        lax.fori_loop(0, 4, gather, 0)
         for h in range(2):
             b4 = WT[2, h, b, 0:1, :] > 0.5
             b2 = WT[2, h, b, 1:2, :] > 0.5
             for ri in range(2):
-                settle(ACC, (h, ri), S2, (h, b, ri), b4, b2, 2, 136)
+                settle(ACC, (h, ri), S2, (0, h, b, ri), b4, b2, 2, 136)
         w = [[WT[2, h, b, k:k + 1, :] for k in (2, 3, 4)] for h in range(2)]
         for first in range(0, 128, 16):
-            re = three(S2, (0, b, 0), first, w[0]) + three(S2, (1, b, 0), first, w[1])
-            im = three(S2, (0, b, 1), first, w[0]) + three(S2, (1, b, 1), first, w[1])
+            re = three(S2, (0, 0, b, 0), first, w[0]) + three(S2, (0, 1, b, 0), first, w[1])
+            im = three(S2, (0, 0, b, 1), first, w[0]) + three(S2, (0, 1, b, 1), first, w[1])
             re, im = turn(re, im, EM[2, b, 0, first:first + 16, :], EM[2, b, 1, first:first + 16, :])
             FB[0, first:first + 16, :] = re.astype(BF16)
             FB[1, first:first + 16, :] = im.astype(BF16)
@@ -511,10 +552,13 @@
     return pl.pallas_call(
         kernel,
         out_shape=jax.ShapeDtypeStruct((2, 1, 8, 128), F32),
-        in_specs=[pl.BlockSpec(memory_space=pltpu.VMEM)] * 8,
+        in_specs=[pl.BlockSpec(memory_space=pltpu.HBM)] * 8,
         out_specs=pl.BlockSpec(memory_space=pltpu.VMEM),
-        scratch_shapes=[
-            v((8, 2, 160, 128), BF16),
+        scratch_shapes=[v(a.shape, a.dtype) for a in args]
+        + [
+            pltpu.SemaphoreType.DMA((8,)),
+            v((8, 2, 2, 16, 128), BF16),
+            v((8, 2, 2, 16, 128), BF16),
             v((2, 128, 128), BF16),
             v((2, 160, 128), BF16),
             v((2, 48, 128), F32),
@@ -536,12 +580,12 @@
             v((4, 2, 2, 4, 128), F32),
             v((2, 2, 2, 4, 128), F32),
             v((2, 2, 8, 128), F32),
-            v((4, 3, 320, 256), BF16),
-            v((8, 3, 288, 256), BF16),
-            v((16, 2, 288, 256), BF16),
-            v((2, 2, 2, 176, 128), F32),
+            v((3, 4 * 320, 256), BF16),
+            v((3, 8 * 288, 256), BF16),
+            v((2, 16 * 288, 256), BF16),
+            v((2, 2, 2, 2, 176, 128), F32),
             v((2, 176, 128), F32),
-            v((2, 2, 2, 160, 128), F32),
+            v((2, 2, 2, 2, 160, 128), F32),
             v((2, 160, 128), F32),
             v((2, 144, 128), F32),
             v((2, 2, 144, 128), F32),
@@ -553,7 +597,7 @@
             pltpu.SemaphoreType.DMA((32,)),
             pltpu.SemaphoreType.DMA((32,)),
         ],
-        compiler_params=pltpu.CompilerParams(collective_id=0, has_side_effects=True, vmem_limit_bytes=48 * 1024 * 1024),
+        compiler_params=pltpu.CompilerParams(collective_id=0, has_side_effects=True, vmem_limit_bytes=63 * 1024 * 1024),
     )(*args)
 
 

time: 54.4 us -> 42.5 us (0.78)
  the two profiles are of different devices: /device:TPU:61 before, /device:TPU:1 now
where the time goes in v1:
time: 42.5 us; the launch traced here: 42.3 us
  Pallas kernels  41 us (96%)
  local copies, waits for them, and re-layouts  1.3 us (3%)
    pallas_call x1, Pallas kernels, body(): pl.pallas_call(kernel, out_shape=jax.ShapeDtypeStruct((2, 1, 8, 128), F32...  41 us
    unnamed x1, local copies, waits for them, and re-layouts  1.3 us

profile of v1, /device:TPU:1, one launch (start us, length us, event | category | flops | bytes accessed | tf_op | source)
XLA Modules:
  0.0 42.3 jit_solution(8412717367225315909)
XLA Ops:
  0.0 41.0 %shard_map.82 = f32[2,1,8,128]{3,2,1,0:T(8,128)} custom-call(bf16[4,2,256,128]{3,2,1,0:T(8,128)(2,1)} %refs_0_.1, s32[3,2,2,256]{3,2,1,0:T(2,128)} %refs_1_.1, s32[3,2,2,256]{3,2,1,0:T(2,128)} %refs_2_.1, bf16[3,2,2,4,256]{4,3,2,1,0:T(4,128)(2,1)} %refs_3_.1, f32[3,2,2,256]{3,2,1,0:T(2,128)} %refs_4_.1, f32[4,3,2,256]{3,2,1,0:T(2,128)} %refs_5_.1, ...), custom_call_target="tpu_custom_call" | custom-call | tf_op jit(solution)/shard_map/pallas_call | solution.py:552
  41.0 1.3 %copy.10 = f32[2,1,8,128]{3,2,1,0:T(8,128)} copy(f32[2,1,8,128]{3,2,1,0:T(8,128)} %shard_map.82) | data formatting | bytes 16384

commit v2 on v1

--- a/solution.py
+++ b/solution.py
@@ -134,8 +134,8 @@
             for b in range(2):
                 main = turned[:, 128 * b:128 * b + 128]
                 L0[b, 320 * j + 160 * ri + 16:320 * j + 160 * ri + 144, 0:128] = main
-                XS[2 * j + ri, b, 0] = main[0:16]
-                XS[2 * j + ri, b, 1] = main[112:128]
+                XS[0, 2 * j + ri, b] = main[0:16]
+                XS[1, 2 * j + ri, b] = main[112:128]
     for side, first in ((0, 0), (1, 240)):
         edge = sub[:, :, first:first + 16, :].reshape(128, 128)
         PE[side] = lax.dot_general(eye, edge, NT, preferred_element_type=F32).astype(BF16)
@@ -171,12 +171,12 @@
 
     @pl.when(X == 0)
     def _():
-        XR[:, :, 0] = jnp.zeros((8, 2, 16, 128), BF16)
+        XR[0] = jnp.zeros((8, 2, 16, 128), BF16)
         PH[:, 0:16, :] = jnp.zeros((2, 16, 128), BF16)
 
     @pl.when(X == 3)
     def _():
-        XR[:, :, 1] = jnp.zeros((8, 2, 16, 128), BF16)
+        XR[1] = jnp.zeros((8, 2, 16, 128), BF16)
         PH[:, 144:160, :] = jnp.zeros((2, 16, 128), BF16)
 
     for side, edge_at in ((0, 0), (1, 3)):
@@ -186,36 +186,6 @@
             TABH[side] = jnp.zeros((SHARED, 128), F32)
             PB1H[side] = jnp.zeros((4, 4, 128), F32)
             PB0H[side] = jnp.zeros((2, 4, 128), F32)
-
-    k_at = row_of((256, 128))
-    near = (jnp.where(k_at < 192, k_at, k_at - 256) - lane_of((256, 128))).astype(F32)
-    for lvl in range(3):
-        r0 = 16 * lvl
-        for b in range(2):
-            for h in range(2):
-                lag = near - TAB[b, r0 + h:r0 + h + 1, :]
-                taps = [TAB[b, r0 + 8 + 4 * h + t:r0 + 9 + 4 * h + t, :] for t in range(4)]
-                RHS[lvl, b, :, 128 * h:128 * h + 128] = tap_matrix(lag, taps).astype(BF16)
-                rows = shift_rows(TAB[b, r0 + 2 + h:r0 + 3 + h, :], TAB[b, r0 + 4 + h:r0 + 5 + h, :])
-                for k, row in enumerate(rows):
-                    WT[lvl, h, b, k:k + 1, :] = row
-
-    def ramp_of(first, lvl):
-        at = X * 128 - ROWS_BELOW_OUT[lvl] + first + row_of((16, 128))
-        inside = jnp.logical_and(at >= 0, at < 512)
-        return at.astype(F32) * (1.0 / 512) - 0.5, inside
-
-    def swing(i, carry):
-        first = pl.multiple_of(i * 16, 16)
-        for lvl in range(3):
-            ramp, inside = ramp_of(first, lvl)
-            for b in range(2):
-                cs = cos_sin(ramp * TAB[b, 16 * lvl + 6:16 * lvl + 7, :])
-                for k in range(2):
-                    EM[lvl, b, k, pl.ds(first, 16), :] = jnp.where(inside, cs[k], 0.0)
-        return carry
-
-    lax.fori_loop(0, 9, swing, 0)
 
     copies = []
     count = [0]
@@ -230,8 +200,8 @@
         ))
         count[0] += 1
 
-    plan(XS.at[:, :, 1], XR.at[:, :, 0], 0, x_ok[1], x_ok[0], rng=X + 1)
-    plan(XS.at[:, :, 0], XR.at[:, :, 1], 1, x_ok[0], x_ok[1], rng=X - 1)
+    plan(XS.at[1], XR.at[0], 0, x_ok[1], x_ok[0], rng=X + 1)
+    plan(XS.at[0], XR.at[1], 1, x_ok[0], x_ok[1], rng=X - 1)
     both = jnp.logical_and
     for side in range(2):
         dy = 1 - 2 * side
@@ -281,6 +251,36 @@
     for send_if, copy in sends:
         pl.when(send_if)(copy.start)
 
+    k_at = row_of((256, 128))
+    near = (jnp.where(k_at < 192, k_at, k_at - 256) - lane_of((256, 128))).astype(F32)
+    for lvl in range(3):
+        r0 = 16 * lvl
+        for b in range(2):
+            for h in range(2):
+                lag = near - TAB[b, r0 + h:r0 + h + 1, :]
+                taps = [TAB[b, r0 + 8 + 4 * h + t:r0 + 9 + 4 * h + t, :] for t in range(4)]
+                RHS[lvl, b, :, 128 * h:128 * h + 128] = tap_matrix(lag, taps).astype(BF16)
+                rows = shift_rows(TAB[b, r0 + 2 + h:r0 + 3 + h, :], TAB[b, r0 + 4 + h:r0 + 5 + h, :])
+                for k, row in enumerate(rows):
+                    WT[lvl, h, b, k:k + 1, :] = row
+
+    def ramp_of(first, lvl):
+        at = X * 128 - ROWS_BELOW_OUT[lvl] + first + row_of((16, 128))
+        inside = jnp.logical_and(at >= 0, at < 512)
+        return at.astype(F32) * (1.0 / 512) - 0.5, inside
+
+    def swing(i, carry):
+        first = pl.multiple_of(i * 16, 16)
+        for lvl in range(3):
+            ramp, inside = ramp_of(first, lvl)
+            for b in range(2):
+                cs = cos_sin(ramp * TAB[b, 16 * lvl + 6:16 * lvl + 7, :])
+                for k in range(2):
+                    EM[lvl, b, k, pl.ds(first, 16), :] = jnp.where(inside, cs[k], 0.0)
+        return carry
+
+    lax.fori_loop(0, 9, swing, 0)
+
     for _, take_if, copy in copies:
         pl.when(take_if)(copy.wait_recv)
 
@@ -365,7 +365,7 @@
                 halo = jnp.where(left_half, hi, lo).astype(BF16)
                 row = 320 * j + 160 * ri + first
                 edge = first in (0, 144)
-                main = [XR[img, b, first // 144] if edge else L0[b, row:row + 16, 0:128] for b in range(2)]
+                main = [XR[first // 144, img, b] if edge else L0[b, row:row + 16, 0:128] for b in range(2)]
                 lay(L0, row, main[0], main[1], halo, True, edge)
 
     def settle(src, at, dst, to, b4, b2, lvl, rows):
@@ -471,80 +471,72 @@
 
     def rs_copy(k):
         return pltpu.make_async_remote_copy(
-            src_ref=SB.at[k], dst_ref=RS.at[A], send_sem=rs_ssem.at[k], recv_sem=rs_rsem.at[A],
+            src_ref=SB.at[k], dst_ref=RS.at[A], send_sem=rs_ssem, recv_sem=rs_rsem,
             device_id=dict(aper=k), device_id_type=MESH)
 
-    for b in range(2):
-        ACC[...] = jnp.zeros((2, 2, 144, 128), F32)
-
-        def gather(i, carry, b=b):
-            at = pl.multiple_of(i * 1152, 1152)
-            got = dot(L2[b, pl.ds(at, 1152), :], RHS[2, b])
+    own_half = A // 16
+    for step in range(2):
+        b = step
+        for i in range(4):
+            got = dot(L2[b, 1152 * i:1152 * i + 1152, :], RHS[2, b])
             for h in range(2):
                 c = [PC2[4 * h + i, b, 0, j:j + 1, :] for j in range(4)]
                 s = [PC2[4 * h + i, b, 1, j:j + 1, :] for j in range(4)]
                 for first in range(0, 136, 8):
-                    re, im = ACC[h, 0, first:first + 8, :], ACC[h, 1, first:first + 8, :]
+                    if i:
+                        re, im = ACC[h, 0, first:first + 8, :], ACC[h, 1, first:first + 8, :]
                     for j in range(4):
                         row = 288 * j + first
                         x = got[row:row + 8, 128 * h:128 * h + 128]
                         y = got[row + 144:row + 152, 128 * h:128 * h + 128]
-                        re = re + (x * c[j] - y * s[j])
-                        im = im + (x * s[j] + y * c[j])
+                        x, y = turn(x, y, c[j], s[j])
+                        re, im = (re + x, im + y) if i or j else (x, y)
                     ACC[h, 0, first:first + 8, :] = re
                     ACC[h, 1, first:first + 8, :] = im
-            return carry
-
-        lax.fori_loop(0, 4, gather, 0)
         for h in range(2):
             b4 = WT[2, h, b, 0:1, :] > 0.5
             b2 = WT[2, h, b, 1:2, :] > 0.5
             for ri in range(2):
-                settle(ACC, (h, ri), S2, (0, h, b, ri), b4, b2, 2, 136)
+                settle(ACC, (h, ri), S2, (step, h, 0, ri), b4, b2, 2, 136)
         w = [[WT[2, h, b, k:k + 1, :] for k in (2, 3, 4)] for h in range(2)]
         for first in range(0, 128, 16):
-            re = three(S2, (0, 0, b, 0), first, w[0]) + three(S2, (0, 1, b, 0), first, w[1])
-            im = three(S2, (0, 0, b, 1), first, w[0]) + three(S2, (0, 1, b, 1), first, w[1])
+            re = three(S2, (step, 0, 0, 0), first, w[0]) + three(S2, (step, 1, 0, 0), first, w[1])
+            im = three(S2, (step, 0, 0, 1), first, w[0]) + three(S2, (step, 1, 0, 1), first, w[1])
             re, im = turn(re, im, EM[2, b, 0, first:first + 16, :], EM[2, b, 1, first:first + 16, :])
             FB[0, first:first + 16, :] = re.astype(BF16)
             FB[1, first:first + 16, :] = im.astype(BF16)
         parts = [lax.dot_general(eye, FB[ri], NT, preferred_element_type=F32).reshape(16, 8, 128) for ri in range(2)]
-        SB[16 * b:16 * b + 16] = jnp.concatenate(parts, axis=1).astype(BF16)
-
-        def send(k, carry):
+        SB[pl.ds(16 * b, 16)] = jnp.concatenate(parts, axis=1).astype(BF16)
+
+        def send(i, carry, b=b):
+            k = 16 * b + i
+
             @pl.when(k != A)
             def _():
                 rs_copy(k).start()
             return carry
 
-        lax.fori_loop(16 * b, 16 * b + 16, send, 0)
+        lax.fori_loop(0, 16, send, 0)
 
     RS[A] = SB[A]
-
-    def arrive(k, total):
-        @pl.when(k != A)
-        def _():
-            pltpu.make_async_remote_copy(
-                src_ref=SB.at[k], dst_ref=RS.at[k], send_sem=rs_ssem.at[k], recv_sem=rs_rsem.at[k],
-                device_id=dict(aper=k), device_id_type=MESH).wait_recv()
-        return total + RS[k].astype(F32)
-
-    total = lax.fori_loop(0, 32, arrive, jnp.zeros((16, 128), F32)) * (1.0 / math.sqrt(128.0))
-    out[0, 0] = total[0:8]
-    out[1, 0] = total[8:16]
 
     for send_if, _, copy in copies:
         pl.when(send_if)(copy.wait_send)
     for send_if, copy in sends:
         pl.when(send_if)(copy.wait_send)
 
-    def sent(k, carry):
-        @pl.when(k != A)
-        def _():
-            rs_copy(k).wait_send()
-        return carry
-
-    lax.fori_loop(0, 32, sent, 0)
+    some = pl.ds(0, 31)
+    everything = pltpu.make_async_remote_copy(
+        src_ref=SB.at[some], dst_ref=RS.at[some], send_sem=rs_ssem, recv_sem=rs_rsem,
+        device_id=dict(aper=(A + 1) % 32), device_id_type=MESH)
+    everything.wait_recv()
+    parts = [RS[k].astype(F32) for k in range(32)]
+    while len(parts) > 1:
+        parts = [parts[k] + parts[k + 1] for k in range(0, len(parts), 2)]
+    total = parts[0] * (1.0 / math.sqrt(128.0))
+    out[0, 0] = total[0:8]
+    out[1, 0] = total[8:16]
+    everything.wait_send()
 
 
 def body(*args):
@@ -557,8 +549,8 @@
         scratch_shapes=[v(a.shape, a.dtype) for a in args]
         + [
             pltpu.SemaphoreType.DMA((8,)),
-            v((8, 2, 2, 16, 128), BF16),
-            v((8, 2, 2, 16, 128), BF16),
+            v((2, 8, 2, 16, 128), BF16),
+            v((2, 8, 2, 16, 128), BF16),
             v((2, 128, 128), BF16),
             v((2, 160, 128), BF16),
             v((2, 48, 128), F32),
@@ -594,8 +586,8 @@
             v((32, 16, 128), BF16),
             pltpu.SemaphoreType.DMA((48,)),
             pltpu.SemaphoreType.DMA((48,)),
-            pltpu.SemaphoreType.DMA((32,)),
-            pltpu.SemaphoreType.DMA((32,)),
+            pltpu.SemaphoreType.DMA,
+            pltpu.SemaphoreType.DMA,
         ],
         compiler_params=pltpu.CompilerParams(collective_id=0, has_side_effects=True, vmem_limit_bytes=63 * 1024 * 1024),
     )(*args)

time: 42.5 us -> 41.1 us (0.967)
  Pallas kernels: 41 us -> 39.6 us
    pallas_call x1, Pallas kernels: 41 us -> 39.6 us  [body(): pl.pallas_call(kernel, out_shape=jax.ShapeDtypeStruct((2, 1, 8, 128), F32...]
where the time goes in v2:
time: 41.1 us; the launch traced here: 40.9 us
  Pallas kernels  39.6 us (96%)
  local copies, waits for them, and re-layouts  1.3 us (3%)
    pallas_call x1, Pallas kernels, body(): pl.pallas_call(kernel, out_shape=jax.ShapeDtypeStruct((2, 1, 8, 128), F32...  39.6 us
    unnamed x1, local copies, waits for them, and re-layouts  1.3 us

profile of v2, /device:TPU:1, one launch (start us, length us, event | category | flops | bytes accessed | tf_op | source)
XLA Modules:
  0.0 40.9 jit_solution(15866011000437105902)
XLA Ops:
  0.0 39.6 %shard_map.82 = f32[2,1,8,128]{3,2,1,0:T(8,128)} custom-call(bf16[4,2,256,128]{3,2,1,0:T(8,128)(2,1)} %refs_0_.1, s32[3,2,2,256]{3,2,1,0:T(2,128)} %refs_1_.1, s32[3,2,2,256]{3,2,1,0:T(2,128)} %refs_2_.1, bf16[3,2,2,4,256]{4,3,2,1,0:T(4,128)(2,1)} %refs_3_.1, f32[3,2,2,256]{3,2,1,0:T(2,128)} %refs_4_.1, f32[4,3,2,256]{3,2,1,0:T(2,128)} %refs_5_.1, ...), custom_call_target="tpu_custom_call" | custom-call | tf_op jit(solution)/shard_map/pallas_call | solution.py:544
  39.6 1.3 %copy.10 = f32[2,1,8,128]{3,2,1,0:T(8,128)} copy(f32[2,1,8,128]{3,2,1,0:T(8,128)} %shard_map.82) | data formatting | bytes 16384

commit v3 on v2

--- a/solution.py
+++ b/solution.py
@@ -421,7 +421,7 @@
 
         def two_images(i, carry, lvl=lvl, src=src, dst=dst, rows=rows, images=images, width=width, phases=phases):
             for u in range(2):
-                at = pl.multiple_of((2 * i + u) * (2 * rows), 2 * rows)
+                at = (2 * i + u) * (2 * rows)
                 for b in range(2):
                     got = dot(src[b, pl.ds(at, 2 * rows), :], RHS[lvl, b])
                     for h in range(2):
@@ -452,11 +452,12 @@
                             main.append(turn(re, im, turned[h][b][0], turned[h][b][1]))
                         for ri in range(2):
                             halo = pltpu.roll(HB[ri, first:first + 16, :], back[h], 1).astype(BF16)
-                            row = pl.multiple_of((images * h + m) * 288 + 144 * ri + first, 16)
+                            row = (images * h + m) * 288 + 144 * ri + first
                             lay(dst, row, main[0][ri].astype(BF16), main[1][ri].astype(BF16), halo, lvl == 0)
             return carry
 
-        lax.fori_loop(0, images // 2, two_images, 0)
+        for i in range(images // 2):
+            two_images(i, 0)
 
     for take_if, copy in takes[2]:
         pl.when(take_if)(copy.wait_recv)

time: 41.1 us -> 40.7 us (level)
  no operation moved by 1% of the time
where the time goes in v3:
time: 40.7 us; the launch traced here: 40.6 us
  Pallas kernels  39.3 us (97%)
  local copies, waits for them, and re-layouts  1.3 us (3%)
    pallas_call x1, Pallas kernels, body(): pl.pallas_call(kernel, out_shape=jax.ShapeDtypeStruct((2, 1, 8, 128), F32...  39.3 us
    unnamed x1, local copies, waits for them, and re-layouts  1.3 us

profile of v3, /device:TPU:1, one launch (start us, length us, event | category | flops | bytes accessed | tf_op | source)
XLA Modules:
  0.0 40.6 jit_solution(10630156472880048596)
XLA Ops:
  0.0 39.3 %shard_map.82 = f32[2,1,8,128]{3,2,1,0:T(8,128)} custom-call(bf16[4,2,256,128]{3,2,1,0:T(8,128)(2,1)} %refs_0_.1, s32[3,2,2,256]{3,2,1,0:T(2,128)} %refs_1_.1, s32[3,2,2,256]{3,2,1,0:T(2,128)} %refs_2_.1, bf16[3,2,2,4,256]{4,3,2,1,0:T(4,128)(2,1)} %refs_3_.1, f32[3,2,2,256]{3,2,1,0:T(2,128)} %refs_4_.1, f32[4,3,2,256]{3,2,1,0:T(2,128)} %refs_5_.1, ...), custom_call_target="tpu_custom_call" | custom-call | tf_op jit(solution)/shard_map/pallas_call | solution.py:545
  39.3 1.3 %copy.10 = f32[2,1,8,128]{3,2,1,0:T(8,128)} copy(f32[2,1,8,128]{3,2,1,0:T(8,128)} %shard_map.82) | data formatting | bytes 16384
